TPU v7x, 32 devices: a whole 2x2x4 slice. The times are simulated.
32 devices in a mesh: node: 4 (over z), bond: 8 (over y, x, core).
Axes of the slice: x: 2, y: 2, z: 4, core: 2. Of those that a mesh axis runs over, the one named last changes fastest.
Arguments:
- bottom_nodes: float32 [4, 128, 128, 128], P('node', 'bond'), may hold values from -0.046875 to 0.046875
- upper_nodes: float32 [4, 128, 128, 128], P(None, 'bond', 'node'), may hold values from -0.046875 to 0.046875
- leaf_up: float32 [4, 3, 2, 128, 128], P('node'), may hold values from -2 to 3
- outside_env: float32 [3, 128, 128], replicated, may hold values from -2 to 3
- top_env: float32 [3, 128, 128], replicated, may hold values from -2 to 3
Outputs:
- leaf_down: float32 [4, 3, 2, 128, 128], P('node', None, None, 'bond')
- subtree_env: float32 [3, 128, 128], replicated
All inputs are finite; a program needn't handle non-finite values.
Results may differ from a plain program's by a relative error of at most 0.0001.
Values sent between devices are 32-bit elements; how exact they have to be, the bound alone decides.
A program may use at most 128 MiB of HBM per device.

v0:
```python
import jax
import jax.numpy as jnp
from jax import lax
from jax.sharding import PartitionSpec as P

highest = lax.Precision.HIGHEST


def grow_product(tensor, left_env, right_env):
    middle = jnp.einsum("skac,spcd->skpad", left_env, tensor, precision=highest)
    return jnp.einsum("skpad,skbd->skpab", middle, right_env, precision=highest)


def gram_partial(tensor, product):
    return jnp.einsum("spab,skqab->skpq", tensor, product, precision=highest)


def first_part(tensor, worked, right_env):
    first = jnp.einsum("skpcd,skbd->skpcb", worked, right_env, precision=highest)
    return jnp.einsum("spab,skpcb->skac", tensor, first, precision=highest)


def second_part(tensor, worked, left_env):
    second = jnp.einsum("skac,skpcd->skpad", left_env, worked, precision=highest)
    return jnp.einsum("spab,skpad->skbd", tensor, second, precision=highest)


def upper_up(columns, parents, left_env, right_env):
    middle = jnp.einsum("skac,spcd->skpad", left_env, columns, precision=highest)
    middle_rows = lax.all_to_all(middle, "node", split_axis=3, concat_axis=4, tiled=True)
    product = jnp.einsum("skpad,skbd->skpab", middle_rows, right_env, precision=highest)
    product_all = lax.all_to_all(product, "bond", split_axis=4, concat_axis=2, tiled=True)
    return lax.psum(gram_partial(parents, product_all), ("node", "bond"))


def down_parts(columns, parents, above, left_env, right_env, with_second):
    worked_all = jnp.einsum("skpq,sqcd->skpcd", above, parents, precision=highest)
    worked = lax.all_to_all(worked_all, "bond", split_axis=2, concat_axis=4, tiled=True)
    first_rows = jnp.einsum("skpcd,skbd->skpcb", worked, right_env, precision=highest)
    first_cols = lax.all_to_all(first_rows, "node", split_axis=4, concat_axis=3, tiled=True)
    first_env = jnp.einsum("spab,skpcb->skac", columns, first_cols, precision=highest)
    if not with_second:
        return (first_env,)
    side = jnp.einsum("spab,skac->skpcb", columns, left_env, precision=highest)
    side_rows = lax.all_to_all(side, "node", split_axis=3, concat_axis=4, tiled=True)
    second_env = jnp.einsum("skpcb,skpcd->skbd", side_rows, worked, precision=highest)
    return (first_env, second_env)


def local(bottom_nodes, upper_nodes, leaf_up, outside_env, top_env):
    nodes = lax.axis_size("node")
    width = bottom_nodes.shape[2]
    rows = bottom_nodes.shape[1]
    operators = leaf_up.shape[1]
    left_leaf = leaf_up[:, :, 0]
    right_leaf = leaf_up[:, :, 1]
    product = grow_product(bottom_nodes, left_leaf, right_leaf)

    def columns(piece, start):
        return jnp.einsum("skqab,spab->skqp", product, piece, precision=highest)

    transposed = columns(lax.all_gather(bottom_nodes, "bond", axis=1, tiled=True), jnp.int32(0))
    spread = lax.all_gather(transposed, ("node", "bond"), axis=2, tiled=True)
    children = jnp.transpose(spread.reshape(operators, nodes, width, width), (1, 0, 3, 2))
    upper_cols = lax.all_to_all(upper_nodes, "node", split_axis=3, concat_axis=2, tiled=True)
    upper_pars = lax.all_to_all(upper_nodes, "bond", split_axis=3, concat_axis=1, tiled=True)
    ups = {nodes: children}
    level_size = nodes // 2
    while level_size >= 1:
        below = ups[2 * level_size]
        ups[level_size] = upper_up(
            upper_cols[level_size : 2 * level_size],
            upper_pars[level_size : 2 * level_size],
            below[0::2],
            below[1::2],
        )
        level_size = level_size // 2
    root_env = ups[1]
    crown_part = down_parts(
        upper_cols[0:1], upper_pars[0:1], top_env[None], root_env, outside_env[None], False
    )[0]
    above = lax.psum(crown_part, ("node", "bond"))
    level_size = 1
    while level_size < nodes:
        below = ups[2 * level_size]
        first_env, second_env = down_parts(
            upper_cols[level_size : 2 * level_size],
            upper_pars[level_size : 2 * level_size],
            above,
            below[0::2],
            below[1::2],
            True,
        )
        first_env, second_env = lax.psum((first_env, second_env), ("node", "bond"))
        above = jnp.stack([first_env, second_env], 1).reshape(
            2 * level_size, operators, width, width
        )
        level_size = level_size * 2
    mine = lax.dynamic_index_in_dim(above, lax.axis_index("node"), 0, keepdims=True)
    own_rows = lax.dynamic_slice_in_dim(mine, lax.axis_index("bond") * rows, rows, 2)
    worked = jnp.einsum(
        "skpq,sqcd->skpcd",
        own_rows,
        lax.all_gather(bottom_nodes, "bond", axis=1, tiled=True),
        precision=highest,
    )
    first_env = first_part(bottom_nodes, worked, right_leaf)
    second_env = second_part(bottom_nodes, worked, left_leaf)
    first_env, second_env = lax.psum((first_env, second_env), "bond")
    offset = lax.axis_index("bond") * rows
    first_env = lax.dynamic_slice_in_dim(first_env, offset, rows, 2)
    second_env = lax.dynamic_slice_in_dim(second_env, offset, rows, 2)
    leaf_down = jnp.stack([first_env, second_env], 2)
    return (leaf_down, root_env[0])


def solution(mesh):
    placed = (
        P("node", "bond", None, None),
        P(None, "bond", "node", None),
        P("node", None, None, None, None),
        P(),
        P(),
    )
    return jax.shard_map(
        local,
        mesh=mesh,
        in_specs=placed,
        out_specs=(P("node", None, None, "bond", None), P()),
        check_vma=False,
    )
```

profile of v0, /device:TPU:0, one launch (start us, length us, event | category | flops | bytes accessed | tf_op | source)
XLA Modules:
  0.0 1110.4 jit_solution(17119100915857108100)
XLA Ops:
  14.7 4.8 reshape.211
  19.5 5.2 all-to-all-start
  24.7 5.0 reshape.207
  29.7 17.2 %all-to-all-done = f32[8,1,32768]{2,1,0:T(1,128)S(1)} async-done(((f32[8,1,32768]{2,1,0:T(1,128)}), f32[8,1,32768]{2,1,0:T(1,128)S(1)}, u32[]{:S(2)}, u32[]{:S(2)}) %all-to-all-start) | async-done | bytes 1048608 | tf_op jit(solution)/shard_map/all_to_all | solution.py:66
  46.9 4.6 all-to-all-start.3
  51.5 5.1 convolution_bitcast_fusion
  59.5 5.3 fusion.48
  73.1 4.6 copy.88
  86.5 4.6 all-to-all-start.1
  91.1 4.6 reduce
  99.2 4.9 copy.231
  110.8 11.0 fusion.19
  121.8 44.7 %all-gather = f32[3,512,128]{2,1,0:T(8,128)S(1)} all-gather(f32[3,16,128]{2,1,0:T(8,128)S(1)} %fusion.19), channel_id=2, replica_groups=mesh['node'=4,'bond'=8] {'node','bond'}, dimensions={1}, use_global_device_ids=true | all-gather | bytes 811008 | tf_op jit(solution)/shard_map/all_gather | solution.py:63
  169.6 6.1 copy.111
  175.6 5.9 reshape.213
  185.9 4.6 reduce.5
  193.9 5.9 convolution_bitcast_fusion.5
  204.4 19.3 %all-to-all-done.5 = f32[4,1,98304]{2,1,0:T(1,128)} async-done(((f32[4,1,98304]{2,1,0:T(1,128)}), f32[4,1,98304]{2,1,0:T(1,128)}, u32[]{:S(2)}, u32[]{:S(2)}) %all-to-all-start.5) | async-done | bytes 1572896 | tf_op jit(solution)/shard_map/all_to_all | solution.py:30
  228.2 6.2 reduce.3
  234.3 4.9 reshape.214
  239.2 9.4 copy.230
  248.6 5.3 all_to_all.182
  256.5 7.0 copy.113
  263.5 7.7 reshape.215
  277.5 7.0 copy.136
  284.5 5.9 reshape.209
  290.4 5.5 all-to-all-done.6
  295.9 5.0 all-to-all-start.11
  308.5 4.7 reduce.6
  328.8 4.7 reshape.216
  333.5 6.5 copy.115
  340.0 8.0 fusion.10
  348.6 126.9 %all-reduce.13.cloned.1.call-done = (f32[2,3,128,128]{2,3,1,0:T(8,128)}, f32[3,128,128]{1,2,0:T(8,128)}) async-done(((f32[2,3,128,128]{2,3,1,0:T(8,128)}, f32[3,128,128]{1,2,0:T(8,128)}), (f32[2,3,128,128]{2,3,1,0:T(8,128)}, f32[3,128,128]{1,2,0:T(8,128)})) %all-reduce.13.cloned.1.call-update) | async-done | bytes 589840 | tf_op jit(solution)/shard_map/psum | solution.py:33
  499.2 5.0 all-to-all-start.8
  504.2 4.5 reduce.8
  512.1 6.0 convolution_bitcast_fusion.4
  525.6 5.1 all-to-all-start.7
  541.0 6.9 all-to-all-done.7
  552.2 4.7 reduce.7
  560.7 5.6 copy.233
  570.3 5.7 convolution_bitcast_fusion.15
  576.0 4.7 reduce.9
  591.8 130.3 %all-reduce.11.cloned.1.call-done = (f32[1,1,3,128,128]{3,4,2,1,0:T(8,128)}, f32[1,1,3,128,128]{3,4,2,1,0:T(8,128)}) async-done(((f32[1,1,3,128,128]{3,4,2,1,0:T(8,128)}, f32[1,1,3,128,128]{3,4,2,1,0:T(8,128)}), (f32[1,1,3,128,128]{3,4,2,1,0:T(8,128)}, f32[1,1,3,128,128]{3,4,2,1,0:T(8,128)})) %all-reduce.11.cloned.1.call-update) | async-done | bytes 393232 | tf_op jit(solution)/shard_map/psum | solution.py:94
  724.5 6.1 copy.130
  730.6 7.6 reshape.227
  742.5 4.7 reduce.12
  767.5 5.8 reduce.10
  773.3 4.7 reshape.228
  784.6 9.9 fusion.31
  794.5 6.0 copy.134
  800.4 5.9 reshape.229
  811.0 6.2 reduce.1
  817.1 4.9 reshape.210
  822.0 9.4 copy.228
  831.4 6.2 all_to_all.204
  849.8 8.7 convolution_bitcast_fusion.11
  858.5 6.2 reduce.11
  864.6 4.9 reshape.230
  869.5 9.6 copy.229
  879.1 5.0 all_to_all.200
  887.6 131.8 %all-reduce.9.cloned.1.call-done = (f32[2,1,3,128,128]{3,4,2,0,1:T(8,128)}, f32[2,1,3,128,128]{3,4,2,0,1:T(8,128)}, f32[3,128,128]{1,2,0:T(8,128)}) async-done(((f32[2,1,3,128,128]{3,4,2,0,1:T(8,128)}, f32[2,1,3,128,128]{3,4,2,0,1:T(8,128)}, f32[3,128,128]{1,2,0:T(8,128)}), (f32[2,1,3,128,128]{3,4,2,0,1:T(8,128)}, f32[2,1,3,128,128]{3,4,2,0,1:T(8,128)}, ...) | async-done | bytes 983056 | tf_op jit(solution)/shard_map/psum | solution.py:94
  1020.9 7.9 fusion
  1031.4 6.2 fusion.46
  1047.9 53.5 %all-reduce.15.cloned.1.call-done = (f32[1,3,128,128]{2,3,1,0:T(8,128)}, f32[1,3,128,128]{2,3,1,0:T(8,128)}) async-done(((f32[1,3,128,128]{2,3,1,0:T(8,128)}, f32[1,3,128,128]{2,3,1,0:T(8,128)}), (f32[1,3,128,128]{2,3,1,0:T(8,128)}, f32[1,3,128,128]{2,3,1,0:T(8,128)})) %all-reduce.15.cloned.1.call-update) | async-done | bytes 393232 | tf_op jit(solution)/shard_map/psum | solution.py:109
  (181 shorter events, 227.9 us)
Async XLA Ops:
  7.2 73.3 %copy-start = (f32[3,128,128]{2,1,0:T(8,128)S(1)}, f32[3,128,128]{2,1,0:T(8,128)}, u32[]{:S(2)}) copy-start(f32[3,128,128]{2,1,0:T(8,128)} %param.9) | copy-start | bytes 589828
  7.2 3.0 copy-start.28
  7.2 103.6 %all-gather.3.cloned.1.call-start = ((), (), s32[]{:S(2)}) async-start(), calls=%async_computation.14 | async-start | bytes 9437184 | tf_op jit(solution)/shard_map/all_gather | solution.py:62
  19.5 27.4 %all-to-all-start = ((f32[8,1,32768]{2,1,0:T(1,128)}), f32[8,1,32768]{2,1,0:T(1,128)S(1)}, u32[]{:S(2)}, u32[]{:S(2)}) async-start(f32[8,1,32768]{2,1,0:T(1,128)} %reshape.211), calls=%async_computation | async-start | bytes 2097152 | tf_op jit(solution)/shard_map/all_to_all | solution.py:66
  24.7 26.8 %copy-start.5 = (f32[1,16,128,128]{3,2,1,0:T(8,128)S(1)}, f32[1,16,128,128]{3,2,1,0:T(8,128)}, u32[]{:S(2)}) copy-start(f32[1,16,128,128]{3,2,1,0:T(8,128)} %param.5) | copy-start | bytes 3145732
  24.7 26.8 %copy-start.24 = (f32[1,3,2,128,128]{4,3,2,1,0:T(8,128)S(1)}, f32[1,3,2,128,128]{4,3,2,1,0:T(8,128)}, u32[]{:S(2)}) copy-start(f32[1,3,2,128,128]{4,3,2,1,0:T(8,128)} %param.7) | copy-start | bytes 1179652
  46.9 4.6 copy-start.18
  46.9 39.6 %all-to-all-start.3 = ((f32[4,1,65536]{2,1,0:T(1,128)}), f32[4,1,65536]{2,1,0:T(1,128)}, u32[]{:S(2)}, u32[]{:S(2)}) async-start(f32[4,1,65536]{2,1,0:T(1,128)} %reshape.207), calls=%async_computation.3 | async-start | bytes 2097152 | tf_op jit(solution)/shard_map/all_to_all | solution.py:65
  77.7 2.3 copy-start.3
  86.5 95.1 %all-to-all-start.1 = ((f32[8,1,24576]{2,1,0:T(1,128)}), f32[8,1,24576]{2,1,0:T(1,128)}, u32[]{:S(2)}, u32[]{:S(2)}) async-start(f32[8,1,24576]{2,1,0:T(1,128)} %reshape.219), calls=%async_computation.1 | async-start | bytes 1572864 | tf_op jit(solution)/shard_map/all_to_all | solution.py:38
  104.1 2.0 copy-start.4
  106.1 4.8 copy-start.7
  166.8 8.8 copy-start.8
  181.6 42.2 %all-to-all-start.5 = ((f32[4,1,98304]{2,1,0:T(1,128)}), f32[4,1,98304]{2,1,0:T(1,128)}, u32[]{:S(2)}, u32[]{:S(2)}) async-start(f32[4,1,98304]{2,1,0:T(1,128)} %reshape.213), calls=%async_computation.5 | async-start | bytes 3145728 | tf_op jit(solution)/shard_map/all_to_all | solution.py:30
  192.9 0.9 copy-start.30
  223.7 47.5 %all-to-all-start.2 = ((f32[4,1,49152]{2,1,0:T(1,128)}), f32[4,1,49152]{2,1,0:T(1,128)}, u32[]{:S(2)}, u32[]{:S(2)}) async-start(f32[4,1,49152]{2,1,0:T(1,128)} %reshape.221), calls=%async_computation.2 | async-start | bytes 1572864 | tf_op jit(solution)/shard_map/all_to_all | solution.py:40
  248.6 5.3 copy-start.9
  271.2 3.7 copy-start.14
  271.2 24.7 %all-to-all-start.6 = ((f32[8,1,49152]{2,1,0:T(1,128)}), f32[8,1,49152]{2,1,0:T(1,128)S(1)}, u32[]{:S(2)}, u32[]{:S(2)}) async-start(f32[8,1,49152]{2,1,0:T(1,128)} %reshape.215), calls=%async_computation.6 | async-start | bytes 3145728 | tf_op jit(solution)/shard_map/all_to_all | solution.py:32
  295.9 5.2 copy-start.11
  295.9 186.5 %all-to-all-start.11 = ((f32[4,1,98304]{2,1,0:T(1,128)}), f32[4,1,98304]{2,1,0:T(1,128)}, u32[]{:S(2)}, u32[]{:S(2)}) async-start(f32[4,1,98304]{2,1,0:T(1,128)} %reshape.209), calls=%async_computation.11 | async-start | bytes 3145728 | tf_op jit(solution)/shard_map/all_to_all | solution.py:45
  300.9 174.6 %all-reduce.13.cloned.1.call-start = ((), (), s32[]{:S(2)}) async-start(), calls=%async_computation.17 | async-start | bytes 1179648 | tf_op jit(solution)/shard_map/psum | solution.py:33
  319.1 3.2 copy-start.29
  319.1 5.3 copy-start.12
  333.5 6.5 copy-start.16
  340.0 8.0 copy-start.19
  348.6 126.9 %copy-start.20 = (f32[128,32,16]{0,1,2:T(8,128)}, f32[128,32,16]{0,1,2:T(8,128)S(1)}, u32[]{:S(2)}) copy-start(f32[128,32,16]{0,1,2:T(8,128)S(1)} %copy.101) | copy-start | bytes 786436
  482.4 16.8 %all-to-all-start.4 = ((f32[8,1,24576]{2,1,0:T(1,128)}), f32[8,1,24576]{2,1,0:T(1,128)}, u32[]{:S(2)}, u32[]{:S(2)}) async-start(f32[8,1,24576]{2,1,0:T(1,128)} %reshape.223), calls=%async_computation.4 | async-start | bytes 1572864 | tf_op jit(solution)/shard_map/all_to_all | solution.py:38
  488.3 0.7 copy-start.22
  499.2 26.4 %all-to-all-start.8 = ((f32[4,1,49152]{2,1,0:T(1,128)}), f32[4,1,49152]{2,1,0:T(1,128)}, u32[]{:S(2)}, u32[]{:S(2)}) async-start(f32[4,1,49152]{2,1,0:T(1,128)} %reshape.217), calls=%async_computation.8 | async-start | bytes 1572864 | tf_op jit(solution)/shard_map/all_to_all | solution.py:45
  511.1 1.0 copy-start.26
  525.6 22.3 %all-to-all-start.7 = ((f32[4,1,49152]{2,1,0:T(1,128)}), f32[4,1,49152]{2,1,0:T(1,128)}, u32[]{:S(2)}, u32[]{:S(2)}) async-start(f32[4,1,49152]{2,1,0:T(1,128)} %reshape.225), calls=%async_computation.7 | async-start | bytes 1572864 | tf_op jit(solution)/shard_map/all_to_all | solution.py:40
  547.9 190.3 %all-to-all-start.12 = ((f32[4,1,49152]{2,1,0:T(1,128)}), f32[4,1,49152]{2,1,0:T(1,128)}, u32[]{:S(2)}, u32[]{:S(2)}) async-start(f32[4,1,49152]{2,1,0:T(1,128)} %reshape.231), calls=%async_computation.12 | async-start | bytes 1572864 | tf_op jit(solution)/shard_map/all_to_all | solution.py:30
  552.1 170.0 %all-reduce.11.cloned.1.call-start = ((), (), s32[]{:S(2)}) async-start(), calls=%async_computation.16 | async-start | bytes 786432 | tf_op jit(solution)/shard_map/psum | solution.py:94
  586.6 3.1 copy-start.23
  586.6 135.5 %copy-start.17 = (f32[2,128,32,16,1]{1,2,3,4,0:T(8,128)S(1)}, f32[2,128,32,16,1]{1,2,3,4,0:T(8,128)}, u32[]{:S(2)}) copy-start(f32[2,128,32,16,1]{1,2,3,4,0:T(8,128)} %copy.167) | copy-start | bytes 1572868
  738.2 25.3 %all-to-all-start.9 = ((f32[8,1,49152]{2,1,0:T(1,128)}), f32[8,1,49152]{2,1,0:T(1,128)}, u32[]{:S(2)}, u32[]{:S(2)}) async-start(f32[8,1,49152]{2,1,0:T(1,128)} %reshape.227), calls=%async_computation.9 | async-start | bytes 3145728 | tf_op jit(solution)/shard_map/all_to_all | solution.py:38
  753.1 2.9 copy-start.27
  763.6 42.8 %all-to-all-start.13 = ((f32[8,1,24576]{2,1,0:T(1,128)}), f32[8,1,24576]{2,1,0:T(1,128)S(1)}, u32[]{:S(2)}, u32[]{:S(2)}) async-start(f32[8,1,24576]{2,1,0:T(1,128)} %reshape.233), calls=%async_computation.13 | async-start | bytes 1572864 | tf_op jit(solution)/shard_map/all_to_all | solution.py:32
  778.1 6.5 copy-start.10
  781.9 2.7 copy-start.2
  806.4 52.1 %all-to-all-start.10 = ((f32[4,1,98304]{2,1,0:T(1,128)}), f32[4,1,98304]{2,1,0:T(1,128)}, u32[]{:S(2)}, u32[]{:S(2)}) async-start(f32[4,1,98304]{2,1,0:T(1,128)} %reshape.229), calls=%async_computation.10 | async-start | bytes 3145728 | tf_op jit(solution)/shard_map/all_to_all | solution.py:40
  810.7 208.7 %all-reduce.9.cloned.1.call-start = ((), (), s32[]{:S(2)}) async-start(), calls=%async_computation.15 | async-start | bytes 1966080 | tf_op jit(solution)/shard_map/psum | solution.py:94
  843.5 6.4 slice-start
  844.5 1.2 copy-start.21
  844.5 5.3 slice-start.1
  844.8 5.0 copy-start.13
  879.1 5.0 copy-start.15
  887.6 213.9 %all-reduce.15.cloned.1.call-start = ((), (), s32[]{:S(2)}) async-start(), calls=%async_computation.18 | async-start | bytes 786432 | tf_op jit(solution)/shard_map/psum | solution.py:109
  1031.4 6.2 copy-start.25
  1037.6 2.9 copy-start.6
  1040.5 63.0 %copy-start.1 = (f32[3,128,128]{2,1,0:T(8,128)S(1)}, f32[3,128,128]{2,1,0:T(8,128)}, u32[]{:S(2)}) copy-start(f32[3,128,128]{2,1,0:T(8,128)} %param.9) | copy-start | bytes 589828
  1043.8 3.3 copy-start.31
Sparse Core Ops, SparseCore 0:
  10.3 69.8 all-gather.2
  348.2 127.2 all-reduce.12
  591.9 130.0 all-reduce.10
  887.7 131.7 all-reduce.8
  1047.2 54.1 all-reduce.14
where the time goes:
time: 1120 us; the launch traced here: 1110 us
  waiting for transfers between devices  496 us (44%)
  local copies, waits for them, and re-layouts  298 us (27%)
  matrix products  122 us (11%)
  other arithmetic  70.6 us (6%)
  starting transfers between devices  63.5 us (6%)
  blocking collectives  44.7 us (4%)
  between operations  15 us (1%)
    psum x2, waiting for transfers between devices, local(): first_env, second_env = lax.psum((first_env, second_env), ('node', 'bond'))  262 us
    unnamed x100, local copies, waits for them, and re-layouts  128 us
    psum x1, waiting for transfers between devices, upper_up(): return lax.psum(gram_partial(parents, product_all), ('node', 'bond'))  127 us
    psum x1, waiting for transfers between devices, local(): first_env, second_env = lax.psum((first_env, second_env), 'bond')  53.5 us
    all_gather x1, blocking collectives, local(): spread = lax.all_gather(transposed, ('node', 'bond'), axis=2, tiled=True)  44.7 us
  transfers between devices with their start and end apart: 19, of which 10 were waited for; matrix products, arithmetic and copies ran while one was open for 37% of the time, Pallas kernels for 0%

commit v1 on v0

v1 whole, which is shorter than its diff:
```python
import functools

import jax
import jax.numpy as jnp
from jax import lax
from jax.experimental import pallas as pl
from jax.experimental.pallas import tpu as pltpu
from jax.sharding import PartitionSpec as P

MESH = pl.DeviceIdType.MESH
NN = (((1,), (0,)), ((), ()))
NT = (((1,), (1,)), ((), ()))
f32 = jnp.float32


def split(x):
    high = x.astype(jnp.bfloat16)
    return high, (x - high.astype(f32)).astype(jnp.bfloat16)


def mm(a, b, dims):
    def dot(u, v):
        return lax.dot_general(u, v, dims, preferred_element_type=f32)

    return dot(a[0], b[0]) + (dot(a[0], b[1]) + dot(a[1], b[0]))


def loop(start, stop, body):
    def step(i, carry):
        body(i)
        return carry

    lax.fori_loop(start, stop, step, 0)


def kernel(
    nodes, bonds,
    bottom, upper, leaf, outside, top,
    leaf_out, root_out,
    all_low, all_up, own_up, grown, worked, side_r, side_l, childs, gram_s, part, got, above, above_s, root,
    far_s, near_s, piece_r, swap_s, swap_r, child_s, child_r, sum_s, sum_r, env_s, env_r, root_s, root_r,
):
    z, j = lax.axis_index("node"), lax.axis_index("bond")
    me = z * bonds + j
    total = nodes * bonds
    chips = bonds // 2
    twin = j + 1 - 2 * lax.rem(j, 2)
    rows, width = bottom.shape[1], bottom.shape[2]
    ops = leaf.shape[1]
    cols = upper.shape[2]
    block = rows * width
    packed = ops * rows
    mine = pl.ds(pl.multiple_of(j * rows, rows), rows)

    def remote(src, dst, send, recv, plane, bond):
        return pltpu.make_async_remote_copy(
            src_ref=src, dst_ref=dst, send_sem=send, recv_sem=recv,
            device_id=(plane, bond), device_id_type=MESH,
        )

    barrier = pltpu.get_barrier_semaphore()

    def greet(m):
        t = lax.rem(me + m, total)
        pl.semaphore_signal(barrier, inc=1, device_id=(t // bonds, lax.rem(t, bonds)), device_id_type=MESH)

    loop(1, total, greet)

    def turn(src, dst):
        def one(p):
            dst[pl.ds(j * block + p, width, stride=rows), :] = src[p]

        loop(0, rows, one)

    turn(bottom.at[0], all_low)
    pl.semaphore_wait(barrier, total - 1)

    def piece(whole, i):
        return whole.at[pl.ds(pl.multiple_of(i * block, block), block), :]

    def far_copy(g, whole, m):
        return remote(piece(whole, j), piece(whole, j), far_s.at[g, m], piece_r.at[g, j], z, lax.rem(j + 2 * m, bonds))

    def near_copy(g, whole, m):
        i = lax.rem(j + 2 * m, bonds)
        return remote(piece(whole, i), piece(whole, i), near_s.at[g, m], piece_r.at[g, i], z, twin)

    def arrived(g, whole, i):
        remote(piece(whole, i), piece(whole, i), far_s.at[g, 0], piece_r.at[g, i], z, twin).wait_recv()

    def gather_start(g, whole):
        loop(1, chips, lambda m: far_copy(g, whole, m).start())
        near_copy(g, whole, 0).start()

    def gather_pass(g, whole):
        def one(m):
            arrived(g, whole, lax.rem(j + 2 * m, bonds))
            near_copy(g, whole, m).start()

        loop(1, chips, one)

    def gather_end(g, whole):
        loop(0, chips, lambda m: arrived(g, whole, lax.rem(twin + 2 * m, bonds)))

    def gather_sent(g, whole):
        loop(1, chips, lambda m: far_copy(g, whole, m).wait_send())
        loop(0, chips, lambda m: near_copy(g, whole, m).wait_send())

    gather_start(0, all_low)

    def swap(m):
        t = lax.rem(z + m, nodes)
        return remote(
            upper.at[t], own_up.at[:, pl.ds(pl.multiple_of(z * cols, cols), cols), :],
            swap_s.at[m], swap_r.at[z], t, j,
        )

    loop(1, nodes, lambda m: swap(m).start())

    def keep(p):
        own_up[p, pl.ds(pl.multiple_of(z * cols, cols), cols), :] = upper[z, p]

    loop(0, rows, keep)

    def prepare(g, x_of, left_of, right_of):
        def operator(k):
            left = left_of(k)
            l, lt, r = split(left), split(left.T), split(right_of(k))

            def one(p, carry):
                x = x_of(p)
                u = mm(split(x), r, NN)
                side_r[g, k, p] = u
                side_l[g, k, p] = mm(split(x.T), l, NN)
                grown[pl.ds(k * rows + p, width, stride=packed), :] = mm(lt, split(u), NN)
                return carry

            lax.fori_loop(0, rows, one, 0, unroll=2)

        loop(0, ops, operator)

    def column(whole, c):
        parts = [whole[pl.ds(pl.multiple_of(i * block + c * rows, rows), rows), :] for i in range(bonds)]
        return jnp.concatenate(parts, axis=0)

    def at_column(c):
        return pl.ds(pl.multiple_of(c * packed, packed), packed)

    def gram(g, whole):
        def one(c, acc):
            return acc + mm(split(grown[at_column(c), :]), split(column(whole, c)), NT)

        out = lax.fori_loop(0, width, one, jnp.zeros((packed, width), f32), unroll=8)
        gram_s[g] = out.reshape(ops, rows, width)

    def down(g, whole, env):
        e = split(env.reshape(packed, width))

        def one(c, carry):
            worked[at_column(c), :] = mm(e, split(column(whole, c)), NN)
            return carry

        lax.fori_loop(0, width, one, 0, unroll=8)

        def operator(k):
            def inner(p, carry):
                first, second = carry
                w = split(worked[pl.ds(k * rows + p, width, stride=packed), :])
                first = first + mm(split(side_r[g, k, p]), w, NT)
                second = second + mm(split(side_l[g, k, p]), w, NN)
                return first, second

            zero = jnp.zeros((width, width), f32)
            first, second = lax.fori_loop(0, rows, inner, (zero, zero), unroll=2)
            part[g, 0, k] = first
            part[g, 1, k] = second

        loop(0, ops, operator)

    def sum_copy(g, m):
        i = lax.rem(j + m, bonds)
        return remote(
            part.at[g, :, :, pl.ds(pl.multiple_of(i * rows, rows), rows), :], got.at[g, j],
            sum_s.at[g, m], sum_r.at[g, j], z, i,
        )

    def plane_sum(g):
        loop(1, bonds, lambda m: sum_copy(g, m).start())

        def add(m, acc):
            i = lax.rem(j + m, bonds)
            remote(
                part.at[g, :, :, mine, :], got.at[g, i], sum_s.at[g, 0], sum_r.at[g, i], z, twin
            ).wait_recv()
            return acc + got[g, i]

        return lax.fori_loop(1, bonds, add, part[g, :, :, mine, :])

    def child_copy(g, number, i):
        return remote(
            gram_s.at[g], childs.at[lax.rem(number, 2), :, mine, :],
            child_s.at[g, i], child_r.at[lax.rem(number, 2), j], number // 2, i,
        )

    def child_send(g, number):
        def one(i):
            own = (number // 2) * bonds + i == me

            @pl.when(own)
            def _():
                childs[lax.rem(number, 2), :, mine, :] = gram_s[g]

            @pl.when(jnp.logical_not(own))
            def _():
                child_copy(g, number, i).start()

        loop(0, bonds, one)

    def child_sent(g, number):
        def one(i):
            @pl.when((number // 2) * bonds + i != me)
            def _():
                child_copy(g, number, i).wait_send()

        loop(0, bonds, one)

    def child_wait():
        for first in range(2):
            number = 2 * z + first
            plane = jnp.where(number >= nodes, number - nodes, number)

            def one(i):
                @pl.when(plane * bonds + i != me)
                def _():
                    remote(
                        gram_s.at[0], childs.at[first, :, pl.ds(pl.multiple_of(i * rows, rows), rows), :],
                        child_s.at[0, 0], child_r.at[first, i], z, twin,
                    ).wait_recv()

            loop(0, bonds, one)

    def env_target(first):
        number = jnp.where(z == 0, 1, 2 * z + first)
        low = (number >= nodes).astype(jnp.int32)
        return number - low * nodes, low

    def env_copy(first):
        plane, low = env_target(first)
        return remote(above_s.at[first], above.at[low], env_s.at[first], env_r.at[low], plane, j)

    def env_wait(low):
        remote(above_s.at[0], above.at[low], env_s.at[0], env_r.at[low], z, twin).wait_recv()

    prepare(0, lambda p: bottom[0, p], lambda k: leaf[0, k, 0], lambda k: leaf[0, k, 1])

    gather_pass(0, all_low)

    def swapped(m):
        i = lax.rem(z + m, nodes)
        remote(
            upper.at[0], own_up.at[:, pl.ds(pl.multiple_of(i * cols, cols), cols), :],
            swap_s.at[0], swap_r.at[i], lax.rem(z + 1, nodes), j,
        ).wait_recv()

    loop(1, nodes, swapped)
    turn(own_up, all_up)
    gather_start(1, all_up)
    gather_end(0, all_low)
    gram(0, all_low)
    child_send(0, nodes + z)

    gather_pass(1, all_up)
    gather_end(1, all_up)

    @pl.when(z == 0)
    def _():
        childs[0] = outside[...]
        childs[1] = outside[...]
        above[0] = top[:, mine, :]

    @pl.when(z > 0)
    def _():
        child_wait()

    prepare(1, lambda p: own_up[p], lambda k: childs[0, k], lambda k: childs[1, k])

    @pl.when(z > 1)
    def _():
        gram(1, all_up)
        child_send(1, z)

    @pl.when(z > 0)
    def _():
        env_wait(0)

    down(1, all_up, above[0])
    above_s[...] = plane_sum(1)
    for first in range(2):
        plane, low = env_target(first)
        live = jnp.logical_or(z > 0, first == 0)

        @pl.when(jnp.logical_and(live, plane == z))
        def _():
            above[1] = above_s[first]

        @pl.when(jnp.logical_and(live, plane != z))
        def _():
            env_copy(first).start()

    def root_copy(m):
        t = lax.rem(me + m, total)
        return remote(
            gram_s.at[1], root.at[:, mine, :], root_s.at[m], root_r.at[j], t // bonds, lax.rem(t, bonds)
        )

    @pl.when(z == 1)
    def _():
        gram(1, all_up)
        root[:, mine, :] = gram_s[1]
        loop(1, total, lambda m: root_copy(m).start())

    @pl.when((nodes + z) // 2 != z)
    def _():
        env_wait(1)

    down(0, all_low, above[1])
    ours = plane_sum(0)
    for first in range(2):
        for k in range(ops):
            leaf_out[0, k, first] = ours[first, k]

    def root_wait(i):
        @pl.when(bonds + i != me)
        def _():
            remote(
                gram_s.at[1], root.at[:, pl.ds(pl.multiple_of(i * rows, rows), rows), :],
                root_s.at[0], root_r.at[i], z, twin,
            ).wait_recv()

    loop(0, bonds, root_wait)
    root_out[...] = root[...]

    gather_sent(0, all_low)
    gather_sent(1, all_up)
    loop(1, nodes, lambda m: swap(m).wait_send())
    child_sent(0, nodes + z)

    @pl.when(z > 1)
    def _():
        child_sent(1, z)

    for g in range(2):
        loop(1, bonds, lambda m: sum_copy(g, m).wait_send())
    for first in range(2):
        plane, low = env_target(first)

        @pl.when(jnp.logical_and(jnp.logical_or(z > 0, first == 0), plane != z))
        def _():
            env_copy(first).wait_send()

    @pl.when(z == 1)
    def _():
        loop(1, total, lambda m: root_copy(m).wait_send())


def solution(mesh):
    nodes, bonds = mesh.shape["node"], mesh.shape["bond"]

    def local(bottom, upper, leaf, outside, top):
        rows, width = bottom.shape[1], bottom.shape[2]
        ops = leaf.shape[1]
        dma = pltpu.SemaphoreType.DMA
        return pl.pallas_call(
            functools.partial(kernel, nodes, bonds),
            out_shape=(
                jax.ShapeDtypeStruct((1, ops, 2, rows, width), f32),
                jax.ShapeDtypeStruct((ops, width, width), f32),
            ),
            in_specs=[pl.BlockSpec(memory_space=pltpu.VMEM)] * 5,
            out_specs=(pl.BlockSpec(memory_space=pltpu.VMEM),) * 2,
            scratch_shapes=[
                pltpu.VMEM((bonds * rows * width, width), f32),
                pltpu.VMEM((bonds * rows * width, width), f32),
                pltpu.VMEM((rows, width, width), f32),
                pltpu.VMEM((width * ops * rows, width), f32),
                pltpu.VMEM((width * ops * rows, width), f32),
                pltpu.VMEM((2, ops, rows, width, width), f32),
                pltpu.VMEM((2, ops, rows, width, width), f32),
                pltpu.VMEM((2, ops, width, width), f32),
                pltpu.VMEM((2, ops, rows, width), f32),
                pltpu.VMEM((2, 2, ops, width, width), f32),
                pltpu.VMEM((2, bonds, 2, ops, rows, width), f32),
                pltpu.VMEM((2, ops, rows, width), f32),
                pltpu.VMEM((2, ops, rows, width), f32),
                pltpu.VMEM((ops, width, width), f32),
                dma((2, bonds // 2)),
                dma((2, bonds // 2)),
                dma((2, bonds)),
                dma((nodes,)),
                dma((nodes,)),
                dma((2, bonds)),
                dma((2, bonds)),
                dma((2, bonds)),
                dma((2, bonds)),
                dma((2,)),
                dma((2,)),
                dma((nodes * bonds,)),
                dma((bonds,)),
            ],
            compiler_params=pltpu.CompilerParams(
                collective_id=0, has_side_effects=True, vmem_limit_bytes=56 * 1024 * 1024
            ),
        )(bottom, upper, leaf, outside, top)

    placed = (
        P("node", "bond", None, None),
        P(None, "bond", "node", None),
        P("node", None, None, None, None),
        P(),
        P(),
    )
    return jax.shard_map(
        local,
        mesh=mesh,
        in_specs=placed,
        out_specs=(P("node", None, None, "bond", None), P()),
        check_vma=False,
    )
```

time: 1120 us -> 228 us (0.20)
  waiting for transfers between devices: 496 us -> 0 us
  local copies, waits for them, and re-layouts: 298 us -> 3.04 us
  Pallas kernels: 0 us -> 224 us
  matrix products: 122 us -> 0 us
  other arithmetic: 70.6 us -> 0 us
  starting transfers between devices: 63.5 us -> 0 us
  blocking collectives: 44.7 us -> 0 us
  between operations: 15 us -> 0.64 us
    psum x4 -> x0, waiting for transfers between devices: 442 us -> none  [the longest x2 262 us: local(): first_env, second_env = lax.psum((first_env, second_env), ('node', 'bond'))]
    pallas_call x0 -> x1, Pallas kernels: none -> 224 us  [local(): pl.pallas_call(functools.partial(kernel, nodes, bonds), out_shape=(jax.Sh...]
    unnamed x100 -> x2, local copies, waits for them, and re-layouts: 128 us -> 3.04 us
    dot_general x27 -> x0, matrix products: 122 us -> none  [the longest x3 21.8 us: down_parts(): jnp.einsum('skpcd,skbd->skpcb', worked, right_env, precision=highest)]
    all_to_all x21 -> x0, local copies, waits for them, and re-layouts: 84.5 us -> none  [the longest x4 21.9 us: down_parts(): lax.all_to_all(first_rows, 'node', split_axis=4, concat_axis=3, tiled=True)]
    all_to_all x14 -> x0, other arithmetic: 69.4 us -> none  [the longest x3 15.6 us: down_parts(): lax.all_to_all(first_rows, 'node', split_axis=4, concat_axis=3, tiled=True)]
    all_to_all x14 -> x0, starting transfers between devices: 63 us -> none  [the longest x3 13.9 us: down_parts(): lax.all_to_all(first_rows, 'node', split_axis=4, concat_axis=3, tiled=True)]
    all_to_all x14 -> x0, waiting for transfers between devices: 53.5 us -> none  [the longest x2 19.3 us: upper_up(): lax.all_to_all(middle, 'node', split_axis=3, concat_axis=4, tiled=True)]
  transfers between devices with their start and end apart: 19 -> 0, of which waited for: 10 -> 0; matrix products, arithmetic and copies ran while one was open for 37% -> 0% of each run, Pallas kernels for 0% -> 0%
where the time goes in v1:
time: 228 us; the launch traced here: 227 us
  Pallas kernels  224 us (98%)
  local copies, waits for them, and re-layouts  3.04 us (1%)
    pallas_call x1, Pallas kernels, local(): pl.pallas_call(functools.partial(kernel, nodes, bonds), out_shape=(jax.Sh...  224 us

profile of v1, /device:TPU:0, one launch (start us, length us, event | category | flops | bytes accessed | tf_op | source)
XLA Modules:
  0.0 227.3 jit_solution(17090582133968561478)
XLA Ops:
  0.6 223.6 %shard_map.68 = (f32[1,3,2,16,128]{4,3,2,1,0:T(8,128)}, f32[3,128,128]{2,1,0:T(8,128)}) custom-call(f32[1,16,128,128]{3,2,1,0:T(8,128)} %bottom.1, f32[4,16,32,128]{3,2,1,0:T(8,128)} %upper.1, f32[1,3,2,128,128]{4,3,2,1,0:T(8,128)} %leaf.1, f32[3,128,128]{2,1,0:T(8,128)} %outside.1, f32[3,128,128]{2,1,0:T(8,128)} %top.1), custom_call_target="tpu_custom_call" | custom-call | tf_op jit(solution)/shard_map/pallas_call | solution.py:373
  224.2 1.4 copy.9
  225.7 1.6 copy.10

commit v2 on v1

--- a/solution.py
+++ b/solution.py
@@ -18,11 +18,27 @@
     return high, (x - high.astype(f32)).astype(jnp.bfloat16)
 
 
-def mm(a, b, dims):
-    def dot(u, v):
-        return lax.dot_general(u, v, dims, preferred_element_type=f32)
-
-    return dot(a[0], b[0]) + (dot(a[0], b[1]) + dot(a[1], b[0]))
+def dot(a, b, dims=NN):
+    return lax.dot_general(a, b, dims, preferred_element_type=f32)
+
+
+def wide(x):
+    return jnp.concatenate(split(x), axis=1)
+
+
+def twice(x):
+    w = wide(x)
+    return jnp.concatenate([w, w], axis=0)
+
+
+def halves(out):
+    half = out.shape[1] // 2
+    return out[:, :half] + out[:, half:]
+
+
+def quarters(out):
+    half = out.shape[0] // 2
+    return halves(out[:half] + out[half:])
 
 
 def loop(start, stop, body):
@@ -37,7 +53,7 @@
     nodes, bonds,
     bottom, upper, leaf, outside, top,
     leaf_out, root_out,
-    all_low, all_up, own_up, grown, worked, side_r, side_l, childs, gram_s, part, got, above, above_s, root,
+    all_low, all_up, own_up, grown, worked, side_r, side_l, long_l, long_r, childs, gram_s, part, got, above, above_s, root,
     far_s, near_s, piece_r, swap_s, swap_r, child_s, child_r, sum_s, sum_r, env_s, env_r, root_s, root_r,
 ):
     z, j = lax.axis_index("node"), lax.axis_index("bond")
@@ -122,58 +138,89 @@
 
     loop(0, rows, keep)
 
-    def prepare(g, x_of, left_of, right_of):
-        def operator(k):
-            left = left_of(k)
-            l, lt, r = split(left), split(left.T), split(right_of(k))
-
-            def one(p, carry):
-                x = x_of(p)
-                u = mm(split(x), r, NN)
-                side_r[g, k, p] = u
-                side_l[g, k, p] = mm(split(x.T), l, NN)
-                grown[pl.ds(k * rows + p, width, stride=packed), :] = mm(lt, split(u), NN)
+    def grow(x_of, left_of, right_of):
+        lefts = wide(jnp.concatenate([left_of(k).T for k in range(ops)], axis=0))
+
+        def one(p, carry):
+            out = halves(dot(lefts, twice(x_of(p))))
+            for k in range(ops):
+                grown[pl.ds(k * block + p, width, stride=rows), :] = out[k * width : (k + 1) * width]
+            return carry
+
+        lax.fori_loop(0, rows, one, 0, unroll=2)
+        step = 4 * width
+        for k in range(ops):
+            right = twice(right_of(k))
+
+            def chunk(i, carry):
+                at = pl.ds(pl.multiple_of(k * block + i * step, step), step)
+                grown[at, :] = halves(dot(wide(grown[at, :]), right))
                 return carry
 
-            lax.fori_loop(0, rows, one, 0, unroll=2)
-
-        loop(0, ops, operator)
+            lax.fori_loop(0, block // step, chunk, 0)
+
+    def sides(g, x_of, left_of, right_of):
+        rights = wide(jnp.concatenate([right_of(k).T for k in range(ops)], axis=0))
+
+        def one(p, carry):
+            turned = x_of(p).T
+            out = halves(dot(rights, twice(turned)))
+            turned_wide = wide(turned)
+            at = pl.ds(pl.multiple_of(p * width, width), width)
+            for k in range(ops):
+                side_r[g, k, at, :] = wide(out[k * width : (k + 1) * width])
+                high, low = split(halves(dot(turned_wide, twice(left_of(k)))))
+                side_l[g, k, :width, at] = high
+                side_l[g, k, width:, at] = low
+            return carry
+
+        lax.fori_loop(0, rows, one, 0, unroll=2)
 
     def column(whole, c):
         parts = [whole[pl.ds(pl.multiple_of(i * block + c * rows, rows), rows), :] for i in range(bonds)]
         return jnp.concatenate(parts, axis=0)
 
-    def at_column(c):
-        return pl.ds(pl.multiple_of(c * packed, packed), packed)
-
     def gram(g, whole):
-        def one(c, acc):
-            return acc + mm(split(grown[at_column(c), :]), split(column(whole, c)), NT)
-
-        out = lax.fori_loop(0, width, one, jnp.zeros((packed, width), f32), unroll=8)
-        gram_s[g] = out.reshape(ops, rows, width)
+        def slab(c):
+            parts = [
+                grown[pl.ds(pl.multiple_of(k * block + c * rows, rows), rows), :] for k in range(ops)
+            ]
+            return jnp.concatenate(split(jnp.concatenate(parts, axis=0)), axis=0)
+
+        def one(i, acc):
+            t = jnp.concatenate([slab(2 * i), slab(2 * i + 1)], axis=1)
+            x = jnp.concatenate(
+                [jnp.concatenate(split(column(whole, 2 * i + d)), axis=0) for d in range(2)], axis=1
+            )
+            return acc + dot(t, x, NT)
+
+        zero = jnp.zeros((2 * packed, 2 * width), f32)
+        out = lax.fori_loop(0, width // 2, one, zero, unroll=4)
+        gram_s[g] = quarters(out).reshape(ops, rows, width)
 
     def down(g, whole, env):
-        e = split(env.reshape(packed, width))
+        e = jnp.concatenate(split(env.reshape(packed, width)), axis=0)
 
         def one(c, carry):
-            worked[at_column(c), :] = mm(e, split(column(whole, c)), NN)
+            at = pl.ds(pl.multiple_of(c * packed, packed), packed)
+            worked[at, :] = quarters(dot(e, wide(column(whole, c))))
             return carry
 
         lax.fori_loop(0, width, one, 0, unroll=8)
 
         def operator(k):
-            def inner(p, carry):
-                first, second = carry
-                w = split(worked[pl.ds(k * rows + p, width, stride=packed), :])
-                first = first + mm(split(side_r[g, k, p]), w, NT)
-                second = second + mm(split(side_l[g, k, p]), w, NN)
-                return first, second
-
-            zero = jnp.zeros((width, width), f32)
-            first, second = lax.fori_loop(0, rows, inner, (zero, zero), unroll=2)
-            part[g, 0, k] = first
-            part[g, 1, k] = second
+            def fill(p, carry):
+                high, low = split(worked[pl.ds(k * rows + p, width, stride=packed), :])
+                at = pl.ds(pl.multiple_of(p * width, width), width)
+                long_l[:width, at] = high
+                long_l[width:, at] = low
+                long_r[at, :width] = high
+                long_r[at, width:] = low
+                return carry
+
+            lax.fori_loop(0, rows, fill, 0, unroll=4)
+            part[g, 0, k] = quarters(dot(long_l[...], side_r[g, k])).T
+            part[g, 1, k] = quarters(dot(side_l[g, k], long_r[...]))
 
         loop(0, ops, operator)
 
@@ -251,7 +298,8 @@
     def env_wait(low):
         remote(above_s.at[0], above.at[low], env_s.at[0], env_r.at[low], z, twin).wait_recv()
 
-    prepare(0, lambda p: bottom[0, p], lambda k: leaf[0, k, 0], lambda k: leaf[0, k, 1])
+    grow(lambda p: bottom[0, p], lambda k: leaf[0, k, 0], lambda k: leaf[0, k, 1])
+    sides(0, lambda p: bottom[0, p], lambda k: leaf[0, k, 0], lambda k: leaf[0, k, 1])
 
     gather_pass(0, all_low)
 
@@ -282,12 +330,16 @@
     def _():
         child_wait()
 
-    prepare(1, lambda p: own_up[p], lambda k: childs[0, k], lambda k: childs[1, k])
+    def grow_up():
+        grow(lambda p: own_up[p], lambda k: childs[0, k], lambda k: childs[1, k])
 
     @pl.when(z > 1)
     def _():
+        grow_up()
         gram(1, all_up)
         child_send(1, z)
+
+    sides(1, lambda p: own_up[p], lambda k: childs[0, k], lambda k: childs[1, k])
 
     @pl.when(z > 0)
     def _():
@@ -315,6 +367,7 @@
 
     @pl.when(z == 1)
     def _():
+        grow_up()
         gram(1, all_up)
         root[:, mine, :] = gram_s[1]
         loop(1, total, lambda m: root_copy(m).start())
@@ -384,8 +437,10 @@
                 pltpu.VMEM((rows, width, width), f32),
                 pltpu.VMEM((width * ops * rows, width), f32),
                 pltpu.VMEM((width * ops * rows, width), f32),
-                pltpu.VMEM((2, ops, rows, width, width), f32),
-                pltpu.VMEM((2, ops, rows, width, width), f32),
+                pltpu.VMEM((2, ops, rows * width, 2 * width), jnp.bfloat16),
+                pltpu.VMEM((2, ops, 2 * width, rows * width), jnp.bfloat16),
+                pltpu.VMEM((2 * width, rows * width), jnp.bfloat16),
+                pltpu.VMEM((rows * width, 2 * width), jnp.bfloat16),
                 pltpu.VMEM((2, ops, width, width), f32),
                 pltpu.VMEM((2, ops, rows, width), f32),
                 pltpu.VMEM((2, 2, ops, width, width), f32),

time: 228 us -> 192 us (0.84)
  Pallas kernels: 224 us -> 188 us
    pallas_call x1, Pallas kernels: 224 us -> 188 us  [local(): pl.pallas_call(functools.partial(kernel, nodes, bonds), out_shape=(jax.Sh...]
where the time goes in v2:
time: 192 us; the launch traced here: 191 us
  Pallas kernels  188 us (98%)
  local copies, waits for them, and re-layouts  3.04 us (2%)
    pallas_call x1, Pallas kernels, local(): pl.pallas_call(functools.partial(kernel, nodes, bonds), out_shape=(jax.Sh...  188 us

profile of v2, /device:TPU:0, one launch (start us, length us, event | category | flops | bytes accessed | tf_op | source)
XLA Modules:
  0.0 191.5 jit_solution(1020707380532639617)
XLA Ops:
  0.6 187.8 %shard_map.68 = (f32[1,3,2,16,128]{4,3,2,1,0:T(8,128)}, f32[3,128,128]{2,1,0:T(8,128)}) custom-call(f32[1,16,128,128]{3,2,1,0:T(8,128)} %bottom.1, f32[4,16,32,128]{3,2,1,0:T(8,128)} %upper.1, f32[1,3,2,128,128]{4,3,2,1,0:T(8,128)} %leaf.1, f32[3,128,128]{2,1,0:T(8,128)} %outside.1, f32[3,128,128]{2,1,0:T(8,128)} %top.1), custom_call_target="tpu_custom_call" | custom-call | tf_op jit(solution)/shard_map/pallas_call | solution.py:426
  188.4 1.4 copy.9
  189.8 1.6 copy.10

commit v3 on v2

--- a/solution.py
+++ b/solution.py
@@ -54,7 +54,7 @@
     bottom, upper, leaf, outside, top,
     leaf_out, root_out,
     all_low, all_up, own_up, grown, worked, side_r, side_l, long_l, long_r, childs, gram_s, part, got, above, above_s, root,
-    far_s, near_s, piece_r, swap_s, swap_r, child_s, child_r, sum_s, sum_r, env_s, env_r, root_s, root_r,
+    far_s, near_s, half_s, half_r, piece_r, swap_s, swap_r, child_s, child_r, sum_s, sum_r, env_s, env_r, root_s, root_r,
 ):
     z, j = lax.axis_index("node"), lax.axis_index("bond")
     me = z * bonds + j
@@ -91,36 +91,66 @@
     turn(bottom.at[0], all_low)
     pl.semaphore_wait(barrier, total - 1)
 
-    def piece(whole, i):
-        return whole.at[pl.ds(pl.multiple_of(i * block, block), block), :]
-
-    def far_copy(g, whole, m):
-        return remote(piece(whole, j), piece(whole, j), far_s.at[g, m], piece_r.at[g, j], z, lax.rem(j + 2 * m, bonds))
-
-    def near_copy(g, whole, m):
-        i = lax.rem(j + 2 * m, bonds)
-        return remote(piece(whole, i), piece(whole, i), near_s.at[g, m], piece_r.at[g, i], z, twin)
+    square = chips == 4
+    by_x = j + 2 - 4 * lax.rem(j // 2, 2)
+    turn_y = 4 - 8 * lax.rem(j // 4, 2)
+    by_y, by_xy = j + turn_y, by_x + turn_y
+
+    def piece(whole, i, half=None):
+        if half is None:
+            return whole.at[pl.ds(pl.multiple_of(i * block, block), block), :]
+        size = block // 2
+        return whole.at[pl.ds(pl.multiple_of(i * block + half * size, size), size), :]
+
+    def far_copy(g, whole, m, to):
+        return remote(piece(whole, j), piece(whole, j), far_s.at[g, m], piece_r.at[g, j], z, to)
+
+    def near_copy(g, whole, i):
+        return remote(piece(whole, i), piece(whole, i), near_s.at[g, i // 2], piece_r.at[g, i], z, twin)
+
+    def half_copy(g, whole, i, half, to):
+        return remote(
+            piece(whole, i, half), piece(whole, i, half), half_s.at[g, half], half_r.at[g, half], z, to
+        )
 
     def arrived(g, whole, i):
         remote(piece(whole, i), piece(whole, i), far_s.at[g, 0], piece_r.at[g, i], z, twin).wait_recv()
 
+    def each_far(act):
+        if square:
+            act(1, by_x)
+            act(2, by_y)
+        else:
+            loop(1, chips, lambda m: act(m, lax.rem(j + 2 * m, bonds)))
+
     def gather_start(g, whole):
-        loop(1, chips, lambda m: far_copy(g, whole, m).start())
-        near_copy(g, whole, 0).start()
+        each_far(lambda m, to: far_copy(g, whole, m, to).start())
+        near_copy(g, whole, j).start()
 
     def gather_pass(g, whole):
-        def one(m):
-            arrived(g, whole, lax.rem(j + 2 * m, bonds))
-            near_copy(g, whole, m).start()
-
-        loop(1, chips, one)
+        def one(m, i):
+            arrived(g, whole, i)
+            if square:
+                half_copy(g, whole, i, m - 1, by_y if m == 1 else by_x).start()
+            near_copy(g, whole, i).start()
+
+        each_far(one)
+
+    def gather_last(g, whole):
+        if square:
+            for half in range(2):
+                half_copy(g, whole, by_xy, half, twin).wait_recv()
+            near_copy(g, whole, by_xy).start()
 
     def gather_end(g, whole):
         loop(0, chips, lambda m: arrived(g, whole, lax.rem(twin + 2 * m, bonds)))
 
     def gather_sent(g, whole):
-        loop(1, chips, lambda m: far_copy(g, whole, m).wait_send())
-        loop(0, chips, lambda m: near_copy(g, whole, m).wait_send())
+        each_far(lambda m, to: far_copy(g, whole, m, to).wait_send())
+        if square:
+            half_copy(g, whole, by_x, 0, by_y).wait_send()
+            half_copy(g, whole, by_y, 1, by_x).wait_send()
+        loop(0, chips, lambda m: near_copy(g, whole, lax.rem(j + 2 * m, bonds)).wait_send())
 
     gather_start(0, all_low)
 
@@ -198,6 +228,23 @@
         out = lax.fori_loop(0, width // 2, one, zero, unroll=4)
         gram_s[g] = quarters(out).reshape(ops, rows, width)
 
+    def sum_copy(g, k, m):
+        i = lax.rem(j + m, bonds)
+        return remote(
+            part.at[g, k, :, pl.ds(pl.multiple_of(i * rows, rows), rows), :], got.at[g, k, j],
+            sum_s.at[g, k, m], sum_r.at[g, k, j], z, i,
+        )
+
+    def plane_sum(g, k):
+        def add(m, acc):
+            i = lax.rem(j + m, bonds)
+            remote(
+                part.at[g, k, :, mine, :], got.at[g, k, i], sum_s.at[g, k, 0], sum_r.at[g, k, i], z, twin
+            ).wait_recv()
+            return acc + got[g, k, i]
+
+        return lax.fori_loop(1, bonds, add, part[g, k, :, mine, :])
+
     def down(g, whole, env):
         e = jnp.concatenate(split(env.reshape(packed, width)), axis=0)
 
@@ -219,29 +266,11 @@
                 return carry
 
             lax.fori_loop(0, rows, fill, 0, unroll=4)
-            part[g, 0, k] = quarters(dot(long_l[...], side_r[g, k])).T
-            part[g, 1, k] = quarters(dot(side_l[g, k], long_r[...]))
+            part[g, k, 0] = quarters(dot(long_l[...], side_r[g, k])).T
+            part[g, k, 1] = quarters(dot(side_l[g, k], long_r[...]))
+            loop(1, bonds, lambda m: sum_copy(g, k, m).start())
 
         loop(0, ops, operator)
-
-    def sum_copy(g, m):
-        i = lax.rem(j + m, bonds)
-        return remote(
-            part.at[g, :, :, pl.ds(pl.multiple_of(i * rows, rows), rows), :], got.at[g, j],
-            sum_s.at[g, m], sum_r.at[g, j], z, i,
-        )
-
-    def plane_sum(g):
-        loop(1, bonds, lambda m: sum_copy(g, m).start())
-
-        def add(m, acc):
-            i = lax.rem(j + m, bonds)
-            remote(
-                part.at[g, :, :, mine, :], got.at[g, i], sum_s.at[g, 0], sum_r.at[g, i], z, twin
-            ).wait_recv()
-            return acc + got[g, i]
-
-        return lax.fori_loop(1, bonds, add, part[g, :, :, mine, :])
 
     def child_copy(g, number, i):
         return remote(
@@ -312,41 +341,52 @@
 
     loop(1, nodes, swapped)
     turn(own_up, all_up)
+    gather_last(0, all_low)
     gather_start(1, all_up)
     gather_end(0, all_low)
     gram(0, all_low)
     child_send(0, nodes + z)
 
+    def grow_up():
+        grow(lambda p: own_up[p], lambda k: childs[0, k], lambda k: childs[1, k])
+
+    def sides_up():
+        sides(1, lambda p: own_up[p], lambda k: childs[0, k], lambda k: childs[1, k])
+
     gather_pass(1, all_up)
-    gather_end(1, all_up)
 
     @pl.when(z == 0)
     def _():
         childs[0] = outside[...]
         childs[1] = outside[...]
         above[0] = top[:, mine, :]
-
-    @pl.when(z > 0)
+        sides_up()
+
+    @pl.when(z > 1)
     def _():
         child_wait()
-
-    def grow_up():
-        grow(lambda p: own_up[p], lambda k: childs[0, k], lambda k: childs[1, k])
+        grow_up()
+
+    gather_last(1, all_up)
+    gather_end(1, all_up)
 
     @pl.when(z > 1)
     def _():
-        grow_up()
         gram(1, all_up)
         child_send(1, z)
 
-    sides(1, lambda p: own_up[p], lambda k: childs[0, k], lambda k: childs[1, k])
+    @pl.when(z == 1)
+    def _():
+        child_wait()
 
     @pl.when(z > 0)
     def _():
+        sides_up()
         env_wait(0)
 
     down(1, all_up, above[0])
-    above_s[...] = plane_sum(1)
+    for k in range(ops):
+        above_s[:, k] = plane_sum(1, k)
     for first in range(2):
         plane, low = env_target(first)
         live = jnp.logical_or(z > 0, first == 0)
@@ -377,10 +417,8 @@
         env_wait(1)
 
     down(0, all_low, above[1])
-    ours = plane_sum(0)
-    for first in range(2):
-        for k in range(ops):
-            leaf_out[0, k, first] = ours[first, k]
+    for k in range(ops):
+        leaf_out[0, k] = plane_sum(0, k)
 
     def root_wait(i):
         @pl.when(bonds + i != me)
@@ -403,7 +441,8 @@
         child_sent(1, z)
 
     for g in range(2):
-        loop(1, bonds, lambda m: sum_copy(g, m).wait_send())
+        for k in range(ops):
+            loop(1, bonds, lambda m: sum_copy(g, k, m).wait_send())
     for first in range(2):
         plane, low = env_target(first)
 
@@ -443,20 +482,22 @@
                 pltpu.VMEM((rows * width, 2 * width), jnp.bfloat16),
                 pltpu.VMEM((2, ops, width, width), f32),
                 pltpu.VMEM((2, ops, rows, width), f32),
-                pltpu.VMEM((2, 2, ops, width, width), f32),
-                pltpu.VMEM((2, bonds, 2, ops, rows, width), f32),
+                pltpu.VMEM((2, ops, 2, width, width), f32),
+                pltpu.VMEM((2, ops, bonds, 2, rows, width), f32),
                 pltpu.VMEM((2, ops, rows, width), f32),
                 pltpu.VMEM((2, ops, rows, width), f32),
                 pltpu.VMEM((ops, width, width), f32),
                 dma((2, bonds // 2)),
                 dma((2, bonds // 2)),
+                dma((2, 2)),
+                dma((2, 2)),
                 dma((2, bonds)),
                 dma((nodes,)),
                 dma((nodes,)),
                 dma((2, bonds)),
                 dma((2, bonds)),
-                dma((2, bonds)),
-                dma((2, bonds)),
+                dma((2, ops, bonds)),
+                dma((2, ops, bonds)),
                 dma((2,)),
                 dma((2,)),
                 dma((nodes * bonds,)),

time: 192 us -> 154 us (0.80)
  Pallas kernels: 188 us -> 150 us
    pallas_call x1, Pallas kernels: 188 us -> 150 us  [local(): pl.pallas_call(functools.partial(kernel, nodes, bonds), out_shape=(jax.Sh...]
where the time goes in v3:
time: 154 us
  Pallas kernels  150 us (97%)
  local copies, waits for them, and re-layouts  3.04 us (2%)
    pallas_call x1, Pallas kernels, local(): pl.pallas_call(functools.partial(kernel, nodes, bonds), out_shape=(jax.Sh...  150 us

profile of v3, /device:TPU:0, one launch (start us, length us, event | category | flops | bytes accessed | tf_op | source)
XLA Modules:
  0.0 154.0 jit_solution(5623265435755320090)
XLA Ops:
  0.6 150.3 %shard_map.68 = (f32[1,3,2,16,128]{4,3,2,1,0:T(8,128)}, f32[3,128,128]{2,1,0:T(8,128)}) custom-call(f32[1,16,128,128]{3,2,1,0:T(8,128)} %bottom.1, f32[4,16,32,128]{3,2,1,0:T(8,128)} %upper.1, f32[1,3,2,128,128]{4,3,2,1,0:T(8,128)} %leaf.1, f32[3,128,128]{2,1,0:T(8,128)} %outside.1, f32[3,128,128]{2,1,0:T(8,128)} %top.1), custom_call_target="tpu_custom_call" | custom-call | tf_op jit(solution)/shard_map/pallas_call | solution.py:465
  151.0 1.4 copy.9
  152.4 1.6 %copy.10 = f32[3,128,128]{2,1,0:T(8,128)} copy(f32[3,128,128]{2,1,0:T(8,128)} %get-tuple-element.5) | data formatting | bytes 393216

commit v4 on v3

--- a/solution.py
+++ b/solution.py
@@ -53,7 +53,7 @@
     nodes, bonds,
     bottom, upper, leaf, outside, top,
     leaf_out, root_out,
-    all_low, all_up, own_up, grown, worked, side_r, side_l, long_l, long_r, childs, gram_s, part, got, above, above_s, root,
+    all_low, all_up, own_up, grown, worked, side_r, side_l, long_l, long_r, childs, gram_s, part, got, parts_in, above, root,
     far_s, near_s, half_s, half_r, piece_r, swap_s, swap_r, child_s, child_r, sum_s, sum_r, env_s, env_r, root_s, root_r,
 ):
     z, j = lax.axis_index("node"), lax.axis_index("bond")
@@ -228,32 +228,95 @@
         out = lax.fori_loop(0, width // 2, one, zero, unroll=4)
         gram_s[g] = quarters(out).reshape(ops, rows, width)
 
-    def sum_copy(g, k, m):
+    def band(i):
+        return pl.ds(pl.multiple_of(i * rows, rows), rows)
+
+    def sum_copy(k, m):
         i = lax.rem(j + m, bonds)
         return remote(
-            part.at[g, k, :, pl.ds(pl.multiple_of(i * rows, rows), rows), :], got.at[g, k, j],
-            sum_s.at[g, k, m], sum_r.at[g, k, j], z, i,
-        )
-
-    def plane_sum(g, k):
+            part.at[0, k, :, band(i), :], got.at[k, j], sum_s.at[k, m], sum_r.at[k, j], z, i
+        )
+
+    def plane_sum(k):
         def add(m, acc):
             i = lax.rem(j + m, bonds)
             remote(
-                part.at[g, k, :, mine, :], got.at[g, k, i], sum_s.at[g, k, 0], sum_r.at[g, k, i], z, twin
+                part.at[0, k, :, mine, :], got.at[k, i], sum_s.at[k, 0], sum_r.at[k, i], z, twin
             ).wait_recv()
-            return acc + got[g, k, i]
-
-        return lax.fori_loop(1, bonds, add, part[g, k, :, mine, :])
+            return acc + got[k, i]
+
+        return lax.fori_loop(1, bonds, add, part[0, k, :, mine, :])
+
+    def env_target(first):
+        number = jnp.where(z == 0, 1, 2 * z + first)
+        low = (number >= nodes).astype(jnp.int32)
+        return number - low * nodes, low, jnp.logical_or(z > 0, first == 0)
+
+    def env_copy(k, first, i):
+        plane, low, _ = env_target(first)
+        return remote(
+            part.at[1, k, first, band(i), :], parts_in.at[low, k, j],
+            env_s.at[first, k, i], env_r.at[low, k, j], plane, i,
+        )
+
+    def env_each(k, act, keep_own):
+        for first in range(2):
+            plane, low, live = env_target(first)
+
+            def one(i):
+                own = plane * bonds + i == me
+
+                @pl.when(jnp.logical_and(live, jnp.logical_not(own)))
+                def _():
+                    act(env_copy(k, first, i))
+
+                if keep_own:
+                    @pl.when(jnp.logical_and(live, own))
+                    def _():
+                        parts_in[low, k, j] = part[1, k, first, mine, :]
+
+            loop(0, bonds, one)
+
+    def env_send(k):
+        env_each(k, lambda copy: copy.start(), True)
+
+    def env_sent(k):
+        env_each(k, lambda copy: copy.wait_send(), False)
+
+    def env_wait(low):
+        source = (nodes * low + z) // 2
+
+        def operator(k):
+            def add(i, acc):
+                @pl.when(source * bonds + i != me)
+                def _():
+                    remote(
+                        part.at[1, 0, 0, mine, :], parts_in.at[low, k, i],
+                        env_s.at[0, 0, 0], env_r.at[low, k, i], z, twin,
+                    ).wait_recv()
+
+                return acc + parts_in[low, k, i]
+
+            above[low, k] = lax.fori_loop(0, bonds, add, jnp.zeros((rows, width), f32))
+
+        loop(0, ops, operator)
 
     def down(g, whole, env):
         e = jnp.concatenate(split(env.reshape(packed, width)), axis=0)
-
-        def one(c, carry):
-            at = pl.ds(pl.multiple_of(c * packed, packed), packed)
-            worked[at, :] = quarters(dot(e, wide(column(whole, c))))
+        e = jnp.concatenate([e, e], axis=1)
+
+        def one(i, carry):
+            x = jnp.concatenate(
+                [jnp.concatenate(split(column(whole, 2 * i + d)), axis=0) for d in range(2)], axis=1
+            )
+            out = dot(e, x)
+            out = out[:packed] + out[packed:]
+            at = pl.multiple_of(2 * i * packed, packed)
+            worked[pl.ds(at, packed), :] = out[:, :width]
+            worked[pl.ds(at + packed, packed), :] = out[:, width:]
             return carry
 
-        lax.fori_loop(0, width, one, 0, unroll=8)
+        lax.fori_loop(0, width // 2, one, 0, unroll=4)
 
         def operator(k):
             def fill(p, carry):
@@ -268,7 +331,10 @@
             lax.fori_loop(0, rows, fill, 0, unroll=4)
             part[g, k, 0] = quarters(dot(long_l[...], side_r[g, k])).T
             part[g, k, 1] = quarters(dot(side_l[g, k], long_r[...]))
-            loop(1, bonds, lambda m: sum_copy(g, k, m).start())
+            if g == 0:
+                loop(1, bonds, lambda m: sum_copy(k, m).start())
+            else:
+                env_send(k)
 
         loop(0, ops, operator)
 
@@ -315,22 +381,9 @@
 
             loop(0, bonds, one)
 
-    def env_target(first):
-        number = jnp.where(z == 0, 1, 2 * z + first)
-        low = (number >= nodes).astype(jnp.int32)
-        return number - low * nodes, low
-
-    def env_copy(first):
-        plane, low = env_target(first)
-        return remote(above_s.at[first], above.at[low], env_s.at[first], env_r.at[low], plane, j)
-
-    def env_wait(low):
-        remote(above_s.at[0], above.at[low], env_s.at[0], env_r.at[low], z, twin).wait_recv()
-
     grow(lambda p: bottom[0, p], lambda k: leaf[0, k, 0], lambda k: leaf[0, k, 1])
+    gather_pass(0, all_low)
     sides(0, lambda p: bottom[0, p], lambda k: leaf[0, k, 0], lambda k: leaf[0, k, 1])
-
-    gather_pass(0, all_low)
 
     def swapped(m):
         i = lax.rem(z + m, nodes)
@@ -385,20 +438,6 @@
         env_wait(0)
 
     down(1, all_up, above[0])
-    for k in range(ops):
-        above_s[:, k] = plane_sum(1, k)
-    for first in range(2):
-        plane, low = env_target(first)
-        live = jnp.logical_or(z > 0, first == 0)
-
-        @pl.when(jnp.logical_and(live, plane == z))
-        def _():
-            above[1] = above_s[first]
-
-        @pl.when(jnp.logical_and(live, plane != z))
-        def _():
-            env_copy(first).start()
-
     def root_copy(m):
         t = lax.rem(me + m, total)
         return remote(
@@ -412,13 +451,10 @@
         root[:, mine, :] = gram_s[1]
         loop(1, total, lambda m: root_copy(m).start())
 
-    @pl.when((nodes + z) // 2 != z)
-    def _():
-        env_wait(1)
-
+    env_wait(1)
     down(0, all_low, above[1])
     for k in range(ops):
-        leaf_out[0, k] = plane_sum(0, k)
+        leaf_out[0, k] = plane_sum(k)
 
     def root_wait(i):
         @pl.when(bonds + i != me)
@@ -440,15 +476,9 @@
     def _():
         child_sent(1, z)
 
-    for g in range(2):
-        for k in range(ops):
-            loop(1, bonds, lambda m: sum_copy(g, k, m).wait_send())
-    for first in range(2):
-        plane, low = env_target(first)
-
-        @pl.when(jnp.logical_and(jnp.logical_or(z > 0, first == 0), plane != z))
-        def _():
-            env_copy(first).wait_send()
+    for k in range(ops):
+        loop(1, bonds, lambda m: sum_copy(k, m).wait_send())
+        env_sent(k)
 
     @pl.when(z == 1)
     def _():
@@ -483,8 +513,8 @@
                 pltpu.VMEM((2, ops, width, width), f32),
                 pltpu.VMEM((2, ops, rows, width), f32),
                 pltpu.VMEM((2, ops, 2, width, width), f32),
-                pltpu.VMEM((2, ops, bonds, 2, rows, width), f32),
-                pltpu.VMEM((2, ops, rows, width), f32),
+                pltpu.VMEM((ops, bonds, 2, rows, width), f32),
+                pltpu.VMEM((2, ops, bonds, rows, width), f32),
                 pltpu.VMEM((2, ops, rows, width), f32),
                 pltpu.VMEM((ops, width, width), f32),
                 dma((2, bonds // 2)),
@@ -496,10 +526,10 @@
                 dma((nodes,)),
                 dma((2, bonds)),
                 dma((2, bonds)),
+                dma((ops, bonds)),
+                dma((ops, bonds)),
                 dma((2, ops, bonds)),
                 dma((2, ops, bonds)),
-                dma((2,)),
-                dma((2,)),
                 dma((nodes * bonds,)),
                 dma((bonds,)),
             ],

time: 154 us -> 153 us (level)
  no operation moved by 1% of the time
where the time goes in v4:
time: 153 us
  Pallas kernels  149 us (97%)
  local copies, waits for them, and re-layouts  3.04 us (2%)
    pallas_call x1, Pallas kernels, local(): pl.pallas_call(functools.partial(kernel, nodes, bonds), out_shape=(jax.Sh...  149 us

profile of v4, /device:TPU:0, one launch (start us, length us, event | category | flops | bytes accessed | tf_op | source)
XLA Modules:
  0.0 153.0 jit_solution(14055455472264155897)
XLA Ops:
  0.6 149.4 %shard_map.68 = (f32[1,3,2,16,128]{4,3,2,1,0:T(8,128)}, f32[3,128,128]{2,1,0:T(8,128)}) custom-call(f32[1,16,128,128]{3,2,1,0:T(8,128)} %bottom.1, f32[4,16,32,128]{3,2,1,0:T(8,128)} %upper.1, f32[1,3,2,128,128]{4,3,2,1,0:T(8,128)} %leaf.1, f32[3,128,128]{2,1,0:T(8,128)} %outside.1, f32[3,128,128]{2,1,0:T(8,128)} %top.1), custom_call_target="tpu_custom_call" | custom-call | tf_op jit(solution)/shard_map/pallas_call | solution.py:495
  150.0 1.4 copy.9
  151.4 1.6 %copy.10 = f32[3,128,128]{2,1,0:T(8,128)} copy(f32[3,128,128]{2,1,0:T(8,128)} %get-tuple-element.5) | data formatting | bytes 393216

commit v5 on v4

--- a/solution.py
+++ b/solution.py
@@ -225,7 +225,7 @@
             return acc + dot(t, x, NT)
 
         zero = jnp.zeros((2 * packed, 2 * width), f32)
-        out = lax.fori_loop(0, width // 2, one, zero, unroll=4)
+        out = lax.fori_loop(0, width // 2, one, zero, unroll=16)
         gram_s[g] = quarters(out).reshape(ops, rows, width)
 
     def band(i):
@@ -316,7 +316,7 @@
             worked[pl.ds(at + packed, packed), :] = out[:, width:]
             return carry
 
-        lax.fori_loop(0, width // 2, one, 0, unroll=4)
+        lax.fori_loop(0, width // 2, one, 0, unroll=16)
 
         def operator(k):
             def fill(p, carry):
@@ -328,7 +328,7 @@
                 long_r[at, width:] = low
                 return carry
 
-            lax.fori_loop(0, rows, fill, 0, unroll=4)
+            lax.fori_loop(0, rows, fill, 0, unroll=8)
             part[g, k, 0] = quarters(dot(long_l[...], side_r[g, k])).T
             part[g, k, 1] = quarters(dot(side_l[g, k], long_r[...]))
             if g == 0:
@@ -383,7 +383,6 @@
 
     grow(lambda p: bottom[0, p], lambda k: leaf[0, k, 0], lambda k: leaf[0, k, 1])
     gather_pass(0, all_low)
-    sides(0, lambda p: bottom[0, p], lambda k: leaf[0, k, 0], lambda k: leaf[0, k, 1])
 
     def swapped(m):
         i = lax.rem(z + m, nodes)
@@ -394,8 +393,9 @@
 
     loop(1, nodes, swapped)
     turn(own_up, all_up)
+    gather_start(1, all_up)
+    sides(0, lambda p: bottom[0, p], lambda k: leaf[0, k, 0], lambda k: leaf[0, k, 1])
     gather_last(0, all_low)
-    gather_start(1, all_up)
     gather_end(0, all_low)
     gram(0, all_low)
     child_send(0, nodes + z)

time: 153 us -> 146 us (0.954)
  Pallas kernels: 149 us -> 143 us
    pallas_call x1, Pallas kernels: 149 us -> 143 us  [local(): pl.pallas_call(functools.partial(kernel, nodes, bonds), out_shape=(jax.Sh...]
where the time goes in v5:
time: 146 us
  Pallas kernels  143 us (98%)
  local copies, waits for them, and re-layouts  3.04 us (2%)
    pallas_call x1, Pallas kernels, local(): pl.pallas_call(functools.partial(kernel, nodes, bonds), out_shape=(jax.Sh...  143 us
    unnamed x2, local copies, waits for them, and re-layouts  3.04 us

profile of v5, /device:TPU:0, one launch (start us, length us, event | category | flops | bytes accessed | tf_op | source)
XLA Modules:
  0.0 146.2 jit_solution(8346711534845475293)
XLA Ops:
  0.6 142.5 %shard_map.68 = (f32[1,3,2,16,128]{4,3,2,1,0:T(8,128)}, f32[3,128,128]{2,1,0:T(8,128)}) custom-call(f32[1,16,128,128]{3,2,1,0:T(8,128)} %bottom.1, f32[4,16,32,128]{3,2,1,0:T(8,128)} %upper.1, f32[1,3,2,128,128]{4,3,2,1,0:T(8,128)} %leaf.1, f32[3,128,128]{2,1,0:T(8,128)} %outside.1, f32[3,128,128]{2,1,0:T(8,128)} %top.1), custom_call_target="tpu_custom_call" | custom-call | tf_op jit(solution)/shard_map/pallas_call | solution.py:495
  143.2 1.4 copy.9
  144.6 1.6 %copy.10 = f32[3,128,128]{2,1,0:T(8,128)} copy(f32[3,128,128]{2,1,0:T(8,128)} %get-tuple-element.5) | data formatting | bytes 393216

commit v6 on v5

--- a/solution.py
+++ b/solution.py
@@ -54,7 +54,7 @@
     bottom, upper, leaf, outside, top,
     leaf_out, root_out,
     all_low, all_up, own_up, grown, worked, side_r, side_l, long_l, long_r, childs, gram_s, part, got, parts_in, above, root,
-    far_s, near_s, half_s, half_r, piece_r, swap_s, swap_r, child_s, child_r, sum_s, sum_r, env_s, env_r, root_s, root_r,
+    far_s, near_s, half_s, half_r, early_s, early_r, piece_r, swap_s, swap_r, child_s, child_r, sum_s, sum_r, env_s, env_r, root_s, root_r,
 ):
     z, j = lax.axis_index("node"), lax.axis_index("bond")
     me = z * bonds + j
@@ -123,17 +123,36 @@
         else:
             loop(1, chips, lambda m: act(m, lax.rem(j + 2 * m, bonds)))
 
+    def early_copy(g, whole, m, i, to):
+        at = piece(whole, i, m - 1)
+        return remote(at, at, early_s.at[g, m - 1], early_r.at[g, m - 1], z, to)
+
+    def rest_copy(g, whole, m, i, to):
+        at = piece(whole, i, 2 - m)
+        return remote(at, at, far_s.at[g, m], piece_r.at[g, i], z, to)
+
     def gather_start(g, whole):
-        each_far(lambda m, to: far_copy(g, whole, m, to).start())
+        if square:
+            each_far(lambda m, to: early_copy(g, whole, m, j, to).start())
+            each_far(lambda m, to: rest_copy(g, whole, m, j, to).start())
+        else:
+            each_far(lambda m, to: far_copy(g, whole, m, to).start())
         near_copy(g, whole, j).start()
 
     def gather_pass(g, whole):
+        def pass_on(m, i):
+            early_copy(g, whole, m, i, twin).wait_recv()
+            half_copy(g, whole, i, m - 1, by_y if m == 1 else by_x).start()
+
         def one(m, i):
-            arrived(g, whole, i)
             if square:
-                half_copy(g, whole, i, m - 1, by_y if m == 1 else by_x).start()
+                rest_copy(g, whole, m, i, twin).wait_recv()
+            else:
+                arrived(g, whole, i)
             near_copy(g, whole, i).start()
 
+        if square:
+            each_far(pass_on)
         each_far(one)
 
     def gather_last(g, whole):
@@ -146,7 +165,11 @@
         loop(0, chips, lambda m: arrived(g, whole, lax.rem(twin + 2 * m, bonds)))
 
     def gather_sent(g, whole):
-        each_far(lambda m, to: far_copy(g, whole, m, to).wait_send())
+        if square:
+            each_far(lambda m, to: early_copy(g, whole, m, j, to).wait_send())
+            each_far(lambda m, to: rest_copy(g, whole, m, j, to).wait_send())
+        else:
+            each_far(lambda m, to: far_copy(g, whole, m, to).wait_send())
         if square:
             half_copy(g, whole, by_x, 0, by_y).wait_send()
             half_copy(g, whole, by_y, 1, by_x).wait_send()
@@ -521,6 +544,8 @@
                 dma((2, bonds // 2)),
                 dma((2, 2)),
                 dma((2, 2)),
+                dma((2, 2)),
+                dma((2, 2)),
                 dma((2, bonds)),
                 dma((nodes,)),
                 dma((nodes,)),

time: 146 us -> 146 us (level)
  no operation moved by 1% of the time
where the time goes in v6:
time: 146 us
  Pallas kernels  142 us (97%)
  local copies, waits for them, and re-layouts  3.04 us (2%)
    pallas_call x1, Pallas kernels, local(): pl.pallas_call(functools.partial(kernel, nodes, bonds), out_shape=(jax.Sh...  142 us
    unnamed x2, local copies, waits for them, and re-layouts  3.04 us

profile of v6, /device:TPU:0, one launch (start us, length us, event | category | flops | bytes accessed | tf_op | source)
XLA Modules:
  0.0 145.7 jit_solution(1388612580995831836)
XLA Ops:
  0.6 142.0 %shard_map.68 = (f32[1,3,2,16,128]{4,3,2,1,0:T(8,128)}, f32[3,128,128]{2,1,0:T(8,128)}) custom-call(f32[1,16,128,128]{3,2,1,0:T(8,128)} %bottom.1, f32[4,16,32,128]{3,2,1,0:T(8,128)} %upper.1, f32[1,3,2,128,128]{4,3,2,1,0:T(8,128)} %leaf.1, f32[3,128,128]{2,1,0:T(8,128)} %outside.1, f32[3,128,128]{2,1,0:T(8,128)} %top.1), custom_call_target="tpu_custom_call" | custom-call | tf_op jit(solution)/shard_map/pallas_call | solution.py:518
  142.6 1.4 copy.9
  144.1 1.6 %copy.10 = f32[3,128,128]{2,1,0:T(8,128)} copy(f32[3,128,128]{2,1,0:T(8,128)} %get-tuple-element.5) | data formatting | bytes 393216

commit v7 on v6

--- a/solution.py
+++ b/solution.py
@@ -139,11 +139,15 @@
             each_far(lambda m, to: far_copy(g, whole, m, to).start())
         near_copy(g, whole, j).start()
 
-    def gather_pass(g, whole):
+    def gather_early(g, whole):
         def pass_on(m, i):
             early_copy(g, whole, m, i, twin).wait_recv()
             half_copy(g, whole, i, m - 1, by_y if m == 1 else by_x).start()
 
+        if square:
+            each_far(pass_on)
+
+    def gather_pass(g, whole):
         def one(m, i):
             if square:
                 rest_copy(g, whole, m, i, twin).wait_recv()
@@ -151,8 +155,6 @@
                 arrived(g, whole, i)
             near_copy(g, whole, i).start()
 
-        if square:
-            each_far(pass_on)
         each_far(one)
 
     def gather_last(g, whole):
@@ -405,6 +407,7 @@
             loop(0, bonds, one)
 
     grow(lambda p: bottom[0, p], lambda k: leaf[0, k, 0], lambda k: leaf[0, k, 1])
+    gather_early(0, all_low)
     gather_pass(0, all_low)
 
     def swapped(m):
@@ -420,6 +423,7 @@
     sides(0, lambda p: bottom[0, p], lambda k: leaf[0, k, 0], lambda k: leaf[0, k, 1])
     gather_last(0, all_low)
     gather_end(0, all_low)
+    gather_early(1, all_up)
     gram(0, all_low)
     child_send(0, nodes + z)
 

time: 146 us -> 147 us (level)
  no operation moved by 1% of the time
where the time goes in v7:
time: 147 us
  Pallas kernels  143 us (97%)
  local copies, waits for them, and re-layouts  3.04 us (2%)
    pallas_call x1, Pallas kernels, local(): pl.pallas_call(functools.partial(kernel, nodes, bonds), out_shape=(jax.Sh...  143 us
    unnamed x2, local copies, waits for them, and re-layouts  3.04 us

profile of v7, /device:TPU:0, one launch (start us, length us, event | category | flops | bytes accessed | tf_op | source)
XLA Modules:
  0.0 146.6 jit_solution(10460110049752745534)
XLA Ops:
  0.6 143.0 %shard_map.68 = (f32[1,3,2,16,128]{4,3,2,1,0:T(8,128)}, f32[3,128,128]{2,1,0:T(8,128)}) custom-call(f32[1,16,128,128]{3,2,1,0:T(8,128)} %bottom.1, f32[4,16,32,128]{3,2,1,0:T(8,128)} %upper.1, f32[1,3,2,128,128]{4,3,2,1,0:T(8,128)} %leaf.1, f32[3,128,128]{2,1,0:T(8,128)} %outside.1, f32[3,128,128]{2,1,0:T(8,128)} %top.1), custom_call_target="tpu_custom_call" | custom-call | tf_op jit(solution)/shard_map/pallas_call | solution.py:522
  143.6 1.4 copy.9
  145.0 1.6 %copy.10 = f32[3,128,128]{2,1,0:T(8,128)} copy(f32[3,128,128]{2,1,0:T(8,128)} %get-tuple-element.5) | data formatting | bytes 393216
